TPU v7x, 32 devices: a whole 2x2x4 slice. The times are simulated.
32 devices in a mesh: ctx: 16 (over z, x, core), hd: 2 (over y).
Axes of the slice: x: 2, y: 2, z: 4, core: 2. Of those that a mesh axis runs over, the one named last changes fastest.
Arguments:
- query_rows: bfloat16 [4096, 4096], P('ctx', 'hd'), may hold values from -240 to 240
- key_rows: bfloat16 [4096, 1024], P('ctx', 'hd'), may hold values from -3.5 to 3.5
- value_rows: bfloat16 [4096, 1024], P('ctx', 'hd'), may hold values from -6 to 6
- doc_ids: int32 [64], P('ctx'), may hold values from 0 to 5, never falling along the last dimension, each value on 1 to 40 neighbouring positions
- out_weight: bfloat16 [4096, 4096], P('hd'), may hold values from -0.125 to 0.125
Outputs:
- attended: bfloat16 [4096, 4096], P('ctx', 'hd')
- projected: bfloat16 [4096, 4096], P('ctx', 'hd')
Inputs may be any that keep to these rules, and one draw needn't show every extreme that they name: `doc_ids`: ids never fall along the stretch; each of the 6 documents spans 1 to 40 whole blocks, and one spans exactly 40.
All inputs are finite; a program needn't handle non-finite values.
Results may differ from a plain program's by a relative error of at most 0.019.
Values may be sent and summed in bfloat16 or wider, within the bound.
A program may use at most 64 MiB of HBM per device.

v0:
```python
from functools import partial
import math

import jax
import jax.numpy as jnp
from jax import lax
from jax.sharding import PartitionSpec as P

HDIM = 128
BLOCK = 64


NEG_BIG = -1e30


def attend_part(
    softmax_state, shard_part, leading_row, query_heads, query_pos, query_doc, score_scale
):
    key_part, value_part, doc_part = shard_part
    row_count = key_part.shape[0]
    block_len = 256
    kv_local = query_heads.shape[1]
    key_blocks = key_part.reshape(row_count // block_len, block_len, kv_local, HDIM)
    value_blocks = value_part.reshape(row_count // block_len, block_len, kv_local, HDIM)
    doc_blocks = doc_part.reshape(row_count // block_len, block_len)

    def one_block(block_index, running):
        block_keys = key_blocks[block_index]
        block_values = value_blocks[block_index]
        key_pos = block_index * block_len + jnp.arange(block_len, dtype=jnp.int32)
        visible = (key_pos[None, :] <= query_pos[:, None]) & (key_pos[None, :] >= 0)
        visible = visible & (doc_blocks[block_index][None, :] == query_doc[:, None])

        def compute(inner_state):
            old_max, old_sum, old_weighted = inner_state
            scores = (
                jnp.einsum(
                    "tkgd,skd->kgts", query_heads, block_keys, preferred_element_type=jnp.float32
                )
                * score_scale
            )
            scores = jnp.where(visible[None, None], scores, NEG_BIG)
            new_max = jnp.maximum(old_max, jnp.max(scores, axis=-1))
            factor = jnp.exp(old_max - new_max)
            weights = jnp.where(visible[None, None], jnp.exp(scores - new_max[..., None]), 0.0)
            new_sum = old_sum * factor + jnp.sum(weights, axis=-1)
            update = jnp.einsum(
                "kgts,skd->kgtd",
                weights.astype(jnp.bfloat16),
                block_values,
                preferred_element_type=jnp.float32,
            )
            return (new_max, new_sum, old_weighted * factor[..., None] + update)

        return lax.cond(jnp.any(visible), compute, lambda inner_state: inner_state, running)

    return lax.fori_loop(0, row_count // block_len, one_block, softmax_state)


def attention_part(query_rows, key_rows, value_rows, doc_ids):
    tokens_here = query_rows.shape[0]
    kv_local = key_rows.shape[1] // HDIM
    group_size = query_rows.shape[1] // key_rows.shape[1]
    position = lax.axis_index("ctx")
    query_heads = query_rows.reshape(tokens_here, kv_local, group_size, HDIM)
    query_pos = position * tokens_here + jnp.arange(tokens_here, dtype=jnp.int32)
    token_docs = jnp.repeat(doc_ids, BLOCK)
    fold_part = partial(
        attend_part,
        query_heads=query_heads,
        query_pos=query_pos,
        query_doc=token_docs,
        score_scale=1.0 / math.sqrt(HDIM),
    )
    start_state = (
        jnp.full((kv_local, group_size, tokens_here), NEG_BIG, jnp.float32),
        jnp.zeros((kv_local, group_size, tokens_here), jnp.float32),
        jnp.zeros((kv_local, group_size, tokens_here, HDIM), jnp.float32),
    )
    softmax_state = fold_part(
        start_state,
        (
            lax.all_gather(key_rows, "ctx", axis=0, tiled=True),
            lax.all_gather(value_rows, "ctx", axis=0, tiled=True),
            lax.all_gather(token_docs, "ctx", axis=0, tiled=True),
        ),
        jnp.int32(0),
    )
    final_max, final_sum, final_weighted = softmax_state
    attended = final_weighted / final_sum[..., None]
    return (
        attended.transpose(2, 0, 1, 3)
        .reshape(tokens_here, kv_local * group_size * HDIM)
        .astype(jnp.bfloat16)
    )


def per_device(query_rows, key_rows, value_rows, doc_ids, out_weight):
    attended = attention_part(query_rows, key_rows, value_rows, doc_ids)
    partial_proj = jnp.dot(attended, out_weight, preferred_element_type=jnp.float32)
    projected = lax.psum_scatter(
        partial_proj.astype(jnp.bfloat16), "hd", scatter_dimension=1, tiled=True
    )
    return (attended, projected)


def solution(mesh):
    in_specs = (P("ctx", "hd"), P("ctx", "hd"), P("ctx", "hd"), P("ctx"), P("hd", None))
    out_specs = (P("ctx", "hd"), P("ctx", "hd"))
    return jax.shard_map(
        per_device, mesh=mesh, in_specs=in_specs, out_specs=out_specs, check_vma=False
    )
```

profile of v0, /device:TPU:0, one launch (start us, length us, event | category | flops | bytes accessed | tf_op | source)
XLA Modules:
  0.0 263.8 jit_solution(16964976732616509494)
XLA Ops:
  8.7 1.5 copy.19
  11.0 23.1 %all-gather = s32[16,1,256]{2,1,0:T(1,128)S(1)} all-gather(s32[1,1,256]{2,1,0:T(1,128)S(1)} %reshape.40), channel_id=1, replica_groups=mesh['ctx'=16,'hd'=2] {'ctx'}, dimensions={0}, use_global_device_ids=true | all-gather | bytes 17408 | tf_op jit(solution)/shard_map/all_gather | solution.py:85
  34.1 29.4 %all-gather.4.cloned.1.call-done = bf16[4096,512]{1,0:T(8,128)(2,1)} async-done(((bf16[256,512]{1,0:T(8,128)(2,1)}), bf16[4096,512]{1,0:T(8,128)(2,1)}) %all-gather.4.cloned.1.call-update) | async-done | bytes 4194320 | tf_op jit(solution)/shard_map/all_gather | solution.py:83
  63.5 6.9 %reshape.46 = bf16[16,256,4,128]{3,2,1,0:T(4,128)(2,1)} reshape(bf16[4096,512]{1,0:T(8,128)(2,1)} %all-gather.4.cloned.1.call-done) | data formatting | bytes 8388608 | tf_op jit(solution)/shard_map/reshape | solution.py:23
  70.4 5.4 %copy.21 = bf16[16,256,4,128]{3,1,2,0:T(8,128)(2,1)} copy(bf16[16,256,4,128]{3,2,1,0:T(4,128)(2,1)} %reshape.46) | data formatting | bytes 8388608
  75.8 38.9 %all-gather.6.cloned.1.call-done = bf16[4096,512]{1,0:T(8,128)(2,1)} async-done(((bf16[256,512]{1,0:T(8,128)(2,1)}), bf16[4096,512]{1,0:T(8,128)(2,1)}) %all-gather.6.cloned.1.call-update) | async-done | bytes 4194320 | tf_op jit(solution)/shard_map/all_gather | solution.py:84
  114.7 6.9 %reshape.47 = bf16[16,256,4,128]{3,2,1,0:T(4,128)(2,1)} reshape(bf16[4096,512]{1,0:T(8,128)(2,1)} %all-gather.6.cloned.1.call-done) | data formatting | bytes 8388608 | tf_op jit(solution)/shard_map/reshape | solution.py:24
  121.6 5.3 %copy.23 = bf16[16,256,4,128]{3,1,2,0:T(8,128)(2,1)} copy(bf16[16,256,4,128]{3,2,1,0:T(4,128)(2,1)} %reshape.47) | data formatting | bytes 8388608
  127.2 34.3 %while.18 = (s32[]{:T(128)}, f32[4,4,256]{2,1,0:T(4,128)S(1)}, f32[4,4,256]{2,1,0:T(4,128)S(1)}, f32[4,4,256,128]{3,2,1,0:T(8,128)S(1)}, s32[16,256]{1,0:T(8,128...) while((s32[]{:T(128)}, f32[4,4,256]{2,1,0:T(4,128)S(1)}, ...), condition=%wide.region_6.7_spmd.clone, body=%wide.region_0.6_spmd.clone.sunk | while | flops 551887872 | bytes 18887456 | solution.py:57
  127.4 0.9 fusion.32
  128.9 5.7 %conditional.3 = ((f32[4,4,256]{2,1,0:T(4,128)S(1)}, f32[4,4,256]{2,1,0:T(4,128)S(1)}, f32[4,4,256,128]{3,2,1,0:T(8,128)S(1)})) conditional(s32[]{:T(128)} %convert_element_type.38, (f32[4,4,256]{2,1,0:T(4,128)S(1)}, f32[4,4,256]{2,1,0:T(4,128)S(1)}, f32[4,4,256,128]{3,2,1,0:T(8,128)S(1)}) %tuple.61, (pred[256,256]{0,1:T(8,128)(4,1)S(1)}, ...), branch_computations={%region_2.0_spmd, %region_3.5_spmd} | conditional | flops 551559168 | bytes 18809888 | solution.py:55
  129.0 1.7 fusion.4
  130.7 1.0 fusion.6
  131.8 2.9 %multiply_add_fusion = f32[4,4,256,128]{3,2,1,0:T(8,128)S(1)} fusion(f32[4,4,256,128]{3,2,1,0:T(8,128)S(1)} %get-tuple-element.234, f32[4,256,256,4]{2,1,3,0:T(8,128)S(1)} %get-tuple-element.329, f32[4,4,256]{2,1,0:T(4,128)S(1)} %max.4, pred[256,256]{0,1:T(8,128)(4,1)S(1)} %get-tuple-element.229, f32[4,4,256]{2,1,0:T(4,128)S(1)} %bitcast.51, ...), kind=kOutput, calls=%fused_computation.8 | convolution fusion | flops 274726912 | bytes 8749568 | tf_op jit(solution)/shard_map/while/body/eval_jaxpr/cond/branch_1_fun/kgts,skd->kgtd/dot_general | solution.py:47
  134.9 0.9 fusion.32
  136.7 0.9 fusion.32
  138.4 0.9 fusion.32
  140.2 0.9 fusion.32
  145.6 0.9 fusion.32
  151.0 0.9 fusion.32
  156.3 0.9 fusion.32
  158.1 0.9 fusion.32
  163.9 11.9 %convolution_convert_fusion = bf16[256,4096]{1,0:T(8,128)(2,1)} fusion(bf16[256,2048]{1,0:T(8,128)(2,1)S(1)} %convert_element_type.26, bf16[2048,4096]{1,0:T(8,128)(2,1)} %param.13), kind=kOutput, calls=%fused_computation.31 | convolution fusion | flops 4296015872 | bytes 19922944 | tf_op jit(solution)/shard_map/dot_general | solution.py:100
  175.8 81.5 %reduce-scatter.2.cloned.1.call-done = bf16[256,2048]{1,0:T(8,128)(2,1)} async-done(((bf16[256,4096]{1,0:T(8,128)(2,1)}), bf16[256,2048]{1,0:T(8,128)(2,1)}) %reduce-scatter.2.cloned.1.call-update) | async-done | bytes 1048592 | tf_op jit(solution)/shard_map/reduce_scatter | solution.py:101
  (125 shorter events, 14.1 us)
Async XLA Ops:
  7.2 3.7 %copy-start.1 = (s32[4]{0:T(128)S(1)}, s32[4]{0:T(128)}, u32[]{:S(2)}) copy-start(s32[4]{0:T(128)} %param.12) | copy-start | bytes 52
  7.2 56.3 %all-gather.4.cloned.1.call-start = ((), (), s32[]{:S(2)}) async-start(), calls=%async_computation.1 | async-start | bytes 4456448 | tf_op jit(solution)/shard_map/all_gather | solution.py:83
  7.9 106.8 %all-gather.6.cloned.1.call-start = ((), (), s32[]{:S(2)}) async-start(), calls=%async_computation.2 | async-start | bytes 4456448 | tf_op jit(solution)/shard_map/all_gather | solution.py:84
  8.7 248.6 %reduce-scatter.2.cloned.1.call-start = ((), (), s32[]{:S(2)}) async-start(), calls=%async_computation.3 | async-start | bytes 3145728 | tf_op jit(solution)/shard_map/reduce_scatter | solution.py:101
  163.9 11.9 %copy-start = (bf16[256,2048]{1,0:T(8,128)(2,1)}, bf16[256,2048]{1,0:T(8,128)(2,1)S(1)}, u32[]{:S(2)}) copy-start(bf16[256,2048]{1,0:T(8,128)(2,1)S(1)} %convert_element_type.26) | copy-start | bytes 3145732
Sparse Core Ops, SparseCore 0:
  10.2 53.2 all-gather.3
  65.6 49.0 all-gather.5
  175.9 81.2 reduce-scatter.1
where the time goes:
time: 268 us; the launch traced here: 264 us
  waiting for transfers between devices  151 us (56%)
  local copies, waits for them, and re-layouts  31.4 us (12%)
  blocking collectives  23.1 us (9%)
  matrix products  16.5 us (6%)
  other arithmetic  16 us (6%)
  between operations  13.8 us (5%)
  loops' own time  11.8 us (4%)
    reduce_scatter x1, waiting for transfers between devices, per_device(): lax.psum_scatter(partial_proj.astype(jnp.bfloat16), 'hd', scatter_dimensi...  81.5 us
    all_gather x1, waiting for transfers between devices, attention_part(): lax.all_gather(value_rows, 'ctx', axis=0, tiled=True)  38.9 us
    all_gather x1, waiting for transfers between devices, attention_part(): lax.all_gather(key_rows, 'ctx', axis=0, tiled=True)  29.4 us
    all_gather x1, blocking collectives, attention_part(): lax.all_gather(token_docs, 'ctx', axis=0, tiled=True)  23.1 us
    reduce_or x16, other arithmetic, one_block(): jnp.any(visible)  13.9 us
    unnamed x10, local copies, waits for them, and re-layouts  13 us
    dot_general x1, matrix products, per_device(): jnp.dot(attended, out_weight, preferred_element_type=jnp.float32)  11.9 us
    another operation x1, loops' own time, attend_part(): return lax.fori_loop(0, row_count // block_len, one_block, softmax_state)  11.6 us
  transfers between devices with their start and end apart: 3, of which 3 were waited for; matrix products, arithmetic and copies ran while one was open for 6% of the time, Pallas kernels for 0%

commit v1 on v0

--- a/solution.py
+++ b/solution.py
@@ -4,6 +4,8 @@
 import jax
 import jax.numpy as jnp
 from jax import lax
+from jax.experimental import pallas as pl
+from jax.experimental.pallas import tpu as pltpu
 from jax.sharding import PartitionSpec as P
 
 HDIM = 128
@@ -103,10 +105,276 @@
     )
     return (attended, projected)
 
+NEG_MASK = -1e30
+LOG2E = 1.4426950408889634
+MESH = pl.DeviceIdType.MESH
+
+
+def fused_kernel(
+    levels, reach, q_ref, k_ref, v_ref, doc_ref, w_ref, att_ref, proj_ref,
+    buf, qa, acc, mrow, lrow, wbuf, psend, pown, precv,
+    send_sem, recv_sem, w_sem, ysend_sem, yrecv_sem,
+):
+    rows = q_ref.shape[0]
+    kv_local = k_ref.shape[1] // HDIM
+    group = q_ref.shape[1] // k_ref.shape[1]
+    scale = LOG2E / math.sqrt(HDIM)
+    v_at = rows + 16
+    me = lax.axis_index("ctx")
+    half = lax.axis_index("hd")
+    z, x, c = lax.div(me, 4), lax.rem(lax.div(me, 2), 2), lax.rem(me, 2)
+    up, across, sibling = me + 4, 4 * z + 2 * (1 - x) + c, 4 * z + 2 * x + (1 - c)
+    across_chip = 4 * z + 2 * (1 - x)
+
+    w_copy = pltpu.make_async_copy(w_ref, wbuf, w_sem)
+    w_copy.start()
+
+    barrier = pltpu.get_barrier_semaphore()
+    pl.semaphore_signal(barrier, inc=1, device_id={"ctx": across}, device_id_type=MESH)
+    pl.semaphore_signal(barrier, inc=1, device_id={"ctx": sibling}, device_id_type=MESH)
+    pl.semaphore_signal(barrier, inc=1, device_id={"hd": 1 - half}, device_id_type=MESH)
+
+    @pl.when(z + 1 < levels)
+    def _():
+        pl.semaphore_signal(barrier, inc=1, device_id={"ctx": up}, device_id_type=MESH)
+
+    @pl.when(z > 0)
+    def _():
+        pl.semaphore_signal(barrier, inc=1, device_id={"ctx": me - 4}, device_id_type=MESH)
+
+    buf[me, 0:rows, :] = k_ref[...]
+    buf[me, rows:v_at, :] = doc_ref[...]
+    buf[me, v_at:, :] = v_ref[...]
+
+    pl.semaphore_wait(
+        barrier, 3 + jnp.where(z + 1 < levels, 1, 0) + jnp.where(z > 0, 1, 0)
+    )
+
+    parts = ((0, v_at), (v_at, rows))
+
+    def copy(src, part, direction, target):
+        ref = buf.at[src, pl.ds(parts[part][0], parts[part][1])]
+        return pltpu.make_async_remote_copy(
+            src_ref=ref, dst_ref=ref,
+            send_sem=send_sem.at[direction, src, part],
+            recv_sem=recv_sem.at[src, part],
+            device_id={"ctx": target}, device_id_type=MESH,
+        )
+
+    def sends(src, column):
+        return (
+            (0, up, column & (z + 1 < levels) & (4 * (z + 1) - src <= reach)),
+            (1, across, column & (src < across_chip) & (across_chip - src <= reach)),
+            (2, sibling, (sibling > src) & (sibling - src <= reach)),
+        )
+
+    def forward(src, column, part):
+        for direction, target, needed in sends(src, column):
+            @pl.when(needed)
+            def _():
+                copy(src, part, direction, target).start()
+
+    def drain(src, column):
+        for direction, target, needed in sends(src, column):
+            @pl.when(needed)
+            def _():
+                for part in range(2):
+                    copy(src, part, direction, target).wait_send()
+
+    always = me >= 0
+    for part in range(2):
+        forward(me, always, part)
+
+    lane = lax.broadcasted_iota(jnp.int32, (1, rows), 1)
+    docs = doc_ref[...].astype(jnp.float32)
+    query_doc = jnp.zeros((1, rows), jnp.float32)
+    for b in range(rows // BLOCK):
+        inside = (lane >= b * BLOCK) & (lane < (b + 1) * BLOCK)
+        query_doc = jnp.where(inside, docs[b : b + 1, 0:rows], query_doc)
+    ids = lax.broadcasted_iota(jnp.int32, (HDIM, rows), 0).astype(jnp.float32)
+    onehot = jnp.where(ids == query_doc, 1.0, 0.0).astype(jnp.bfloat16)
+    for kv in range(kv_local):
+        for g in range(group):
+            head = (kv * group + g) * HDIM
+            cols = slice(g * rows, (g + 1) * rows)
+            qa[kv, 0:HDIM, cols] = q_ref[:, head : head + HDIM].T
+            qa[kv, HDIM:, cols] = onehot
+
+    def attend(src, diagonal):
+        shard_docs = buf[src, rows:v_at, 0:HDIM].astype(jnp.float32)
+        doc_lane = lax.broadcasted_iota(jnp.int32, (BLOCK, HDIM), 1).astype(jnp.float32)
+        key_mask = jnp.concatenate(
+            [
+                jnp.where(doc_lane == shard_docs[b : b + 1, :], 0.0, NEG_MASK)
+                for b in range(rows // BLOCK)
+            ],
+            axis=0,
+        ).astype(jnp.bfloat16)
+
+        @pl.loop(0, kv_local)
+        def _(kv):
+            at = pl.ds(pl.multiple_of(kv * HDIM, HDIM), HDIM)
+            keys = jnp.concatenate([buf[src, 0:rows, at], key_mask], axis=1)
+            values = buf[src, v_at:, at]
+            for g in range(group):
+                cols = slice(g * rows, (g + 1) * rows)
+                scores = jnp.dot(keys, qa[kv, :, cols], preferred_element_type=jnp.float32)
+                if diagonal:
+                    key_pos = lax.broadcasted_iota(jnp.int32, scores.shape, 0)
+                    query_pos = lax.broadcasted_iota(jnp.int32, scores.shape, 1)
+                    scores = jnp.where(key_pos <= query_pos, scores, NEG_MASK)
+                top = jnp.max(scores, axis=0, keepdims=True)
+                if not diagonal:
+                    old = mrow[kv, 0:1, cols]
+                    top = jnp.maximum(top, old)
+                    factor = jnp.exp2((old - top) * scale)
+                weights = jnp.exp2((scores - top) * scale)
+                total = jnp.sum(weights, axis=0, keepdims=True)
+                update = lax.dot_general(
+                    values, weights.astype(jnp.bfloat16), (((0,), (0,)), ((), ())),
+                    preferred_element_type=jnp.float32,
+                )
+                if not diagonal:
+                    total = total + lrow[kv, 0:1, cols] * factor
+                    update = update + acc[kv, :, cols] * factor
+                mrow[kv, 0:1, cols] = top
+                lrow[kv, 0:1, cols] = total
+                acc[kv, :, cols] = update
+
+    attend(me, True)
+
+    def event(step):
+        kind = lax.rem(step, 4)
+        back = lax.div(step, 4) - jnp.where(kind >= 2, 1, 0)
+        src_z = z - back
+        src_x = jnp.where(kind >= 2, 1 - x, x)
+        src_c = jnp.where(lax.rem(kind, 2) == 1, 1 - c, c)
+        src = 4 * src_z + 2 * src_x + src_c
+        near = (src < me) & (me - src <= reach)
+        chip = 4 * z + 2 * x
+        by_level = (kind == 0) & (back >= 1) & (4 * z - src <= reach)
+        by_across = (kind == 2) & (src < chip) & (chip - src <= reach)
+        by_sibling = (lax.rem(kind, 2) == 1) & near
+        held = (back >= 0) & (src_z >= 0) & (by_level | by_across | by_sibling)
+        return src, kind, held, held & near
+
+    @pl.loop(0, 4 * (levels + 1))
+    def _(step):
+        src, kind, held, near = event(step)
+
+        @pl.when(held)
+        def _():
+            for part in range(2):
+                copy(src, part, 0, sibling).wait_recv()
+
+                @pl.when(lax.rem(kind, 2) == 0)
+                def _():
+                    forward(src, kind == 0, part)
+
+        @pl.when(near)
+        def _():
+            attend(src, False)
+
+    @pl.loop(0, kv_local)
+    def _(kv):
+        for g in range(group):
+            cols = slice(g * rows, (g + 1) * rows)
+            head = acc[kv, :, cols] / lrow[kv, 0:1, cols]
+            at = pl.ds(pl.multiple_of((kv * group + g) * HDIM, HDIM), HDIM)
+            att_ref[:, at] = head.T.astype(jnp.bfloat16)
+
+    w_copy.wait()
+    chunks, _, width = psend.shape
+
+    def exchange(n):
+        return pltpu.make_async_remote_copy(
+            src_ref=psend.at[n], dst_ref=precv.at[n],
+            send_sem=ysend_sem.at[n], recv_sem=yrecv_sem.at[n],
+            device_id={"hd": 1 - half}, device_id_type=MESH,
+        )
+
+    def project(first, n):
+        at = pl.ds(pl.multiple_of((first * chunks + n) * width, width), width)
+        return jnp.dot(att_ref[...], wbuf[:, at], preferred_element_type=jnp.float32)
+
+    @pl.loop(0, chunks)
+    def _(n):
+        psend[n] = project(1 - half, n).astype(jnp.bfloat16)
+        exchange(n).start()
+
+    @pl.loop(0, chunks)
+    def _(n):
+        pown[n] = project(half, n)
+
+    for n in range(chunks):
+        exchange(n).wait_recv()
+        proj_ref[:, n * width : (n + 1) * width] = (
+            pown[n] + precv[n].astype(jnp.float32)
+        ).astype(jnp.bfloat16)
+
+    for n in range(chunks):
+        exchange(n).wait_send()
+    drain(me, always)
+
+    @pl.loop(0, 4 * (levels + 1))
+    def _(step):
+        src, kind, held, _near = event(step)
+
+        @pl.when(held & (lax.rem(kind, 2) == 0))
+        def _():
+            drain(src, kind == 0)
+
+
+def fused_device(ctx_size, query_rows, key_rows, value_rows, doc_ids, out_weight):
+    rows, q_cols = query_rows.shape
+    kv_cols = key_rows.shape[1]
+    kv_local = kv_cols // HDIM
+    group = q_cols // kv_cols
+    shard_blocks = rows // BLOCK
+    reach = -(-(ctx_size * shard_blocks * 5 // 8 - 1) // shard_blocks)
+    width = 512
+    out_cols = out_weight.shape[1] // 2
+    chunks = out_cols // width
+    doc_tile = jnp.zeros((16, kv_cols), jnp.bfloat16).at[0:shard_blocks].set(
+        jnp.broadcast_to(doc_ids.astype(jnp.bfloat16)[:, None], (shard_blocks, kv_cols))
+    )
+    vmem = pl.BlockSpec(memory_space=pltpu.VMEM)
+    return pl.pallas_call(
+        partial(fused_kernel, ctx_size // 4, reach),
+        out_shape=(
+            jax.ShapeDtypeStruct((rows, q_cols), jnp.bfloat16),
+            jax.ShapeDtypeStruct((rows, out_cols), jnp.bfloat16),
+        ),
+        in_specs=[vmem] * 4 + [pl.BlockSpec(memory_space=pl.ANY)],
+        out_specs=(vmem, vmem),
+        scratch_shapes=[
+            pltpu.VMEM((ctx_size, 2 * rows + 16, kv_cols), jnp.bfloat16),
+            pltpu.VMEM((kv_local, 2 * HDIM, group * rows), jnp.bfloat16),
+            pltpu.VMEM((kv_local, HDIM, group * rows), jnp.float32),
+            pltpu.VMEM((kv_local, 8, group * rows), jnp.float32),
+            pltpu.VMEM((kv_local, 8, group * rows), jnp.float32),
+            pltpu.VMEM(out_weight.shape, jnp.bfloat16),
+            pltpu.VMEM((chunks, rows, width), jnp.bfloat16),
+            pltpu.VMEM((chunks, rows, width), jnp.float32),
+            pltpu.VMEM((chunks, rows, width), jnp.bfloat16),
+            pltpu.SemaphoreType.DMA((3, ctx_size, 2)),
+            pltpu.SemaphoreType.DMA((ctx_size, 2)),
+            pltpu.SemaphoreType.DMA,
+            pltpu.SemaphoreType.DMA((chunks,)),
+            pltpu.SemaphoreType.DMA((chunks,)),
+        ],
+        compiler_params=pltpu.CompilerParams(
+            collective_id=0, has_side_effects=True, vmem_limit_bytes=52 * 1024 * 1024
+        ),
+    )(query_rows, key_rows, value_rows, doc_tile, out_weight)
+
 
 def solution(mesh):
     in_specs = (P("ctx", "hd"), P("ctx", "hd"), P("ctx", "hd"), P("ctx"), P("hd", None))
     out_specs = (P("ctx", "hd"), P("ctx", "hd"))
+    body = per_device
+    if mesh.shape["ctx"] == 16 and mesh.shape["hd"] == 2:
+        body = partial(fused_device, mesh.shape["ctx"])
     return jax.shard_map(
-        per_device, mesh=mesh, in_specs=in_specs, out_specs=out_specs, check_vma=False
-    )
+        body, mesh=mesh, in_specs=in_specs, out_specs=out_specs, check_vma=False
+    )

time: 268 us -> 110 us (0.41)
  the two profiles are of different devices: /device:TPU:0 before, /device:TPU:24 now
where the time goes in v1:
time: 110 us
  Pallas kernels  103 us (94%)
  local copies, waits for them, and re-layouts  5.26 us (5%)
    pallas_call x1, Pallas kernels, fused_device(): pl.pallas_call(partial(fused_kernel, ctx_size // 4, reach), out_shape=(ja...  103 us
    unnamed x6, local copies, waits for them, and re-layouts  5.18 us

profile of v1, /device:TPU:24, one launch (start us, length us, event | category | flops | bytes accessed | tf_op | source)
XLA Modules:
  0.0 109.6 jit_solution(15308352240487706250)
XLA Ops:
  0.6 0.7 convert_element_type.3
  1.3 0.1 scatter.8.doc_ref
  1.4 0.0 copy-start
  1.4 0.9 copy-done
  2.3 0.0 copy-start.1
  2.3 0.9 copy-done.1
  3.3 103.0 %shard_map.68 = (bf16[256,2048]{1,0:T(8,128)(2,1)S(1)}, bf16[256,2048]{1,0:T(8,128)(2,1)}) custom-call(bf16[256,2048]{1,0:T(8,128)(2,1)} %q_ref.1, bf16[256,512]{1,0:T(8,128)(2,1)S(1)} %copy-done, bf16[256,512]{1,0:T(8,128)(2,1)S(1)} %copy-done.1, bf16[16,512]{1,0:T(8,128)(2,1)S(1)} %scatter.8.doc_ref, bf16[2048,4096]{1,0:T(8,128)(2,1)} %w_ref.1), custom_call_target="tpu_custom_call" | custom-call | tf_op jit(solution)/shard_map/pallas_call | solution.py:342
  106.3 1.0 copy.9
  107.3 2.3 %copy.10 = bf16[256,2048]{1,0:T(8,128)(2,1)} copy(bf16[256,2048]{1,0:T(8,128)(2,1)} %get-tuple-element.17) | data formatting | bytes 2097152
  (1 shorter events, 0.0 us)
Async XLA Ops:
  1.4 1.0 copy-start
  2.3 0.9 copy-start.1

commit v2 on v1

--- a/solution.py
+++ b/solution.py
@@ -150,7 +150,10 @@
         barrier, 3 + jnp.where(z + 1 < levels, 1, 0) + jnp.where(z > 0, 1, 0)
     )
 
-    parts = ((0, v_at), (v_at, rows))
+    middle = rows // 2
+    parts = (
+        (0, middle), (middle, v_at - middle), (v_at, middle), (v_at + middle, rows - middle)
+    )
 
     def copy(src, part, direction, target):
         ref = buf.at[src, pl.ds(parts[part][0], parts[part][1])]
@@ -178,11 +181,11 @@
         for direction, target, needed in sends(src, column):
             @pl.when(needed)
             def _():
-                for part in range(2):
+                for part in range(len(parts)):
                     copy(src, part, direction, target).wait_send()
 
     always = me >= 0
-    for part in range(2):
+    for part in range(len(parts)):
         forward(me, always, part)
 
     lane = lax.broadcasted_iota(jnp.int32, (1, rows), 1)
@@ -211,35 +214,48 @@
             axis=0,
         ).astype(jnp.bfloat16)
 
-        @pl.loop(0, kv_local)
-        def _(kv):
-            at = pl.ds(pl.multiple_of(kv * HDIM, HDIM), HDIM)
-            keys = jnp.concatenate([buf[src, 0:rows, at], key_mask], axis=1)
-            values = buf[src, v_at:, at]
-            for g in range(group):
-                cols = slice(g * rows, (g + 1) * rows)
-                scores = jnp.dot(keys, qa[kv, :, cols], preferred_element_type=jnp.float32)
-                if diagonal:
-                    key_pos = lax.broadcasted_iota(jnp.int32, scores.shape, 0)
-                    query_pos = lax.broadcasted_iota(jnp.int32, scores.shape, 1)
-                    scores = jnp.where(key_pos <= query_pos, scores, NEG_MASK)
-                top = jnp.max(scores, axis=0, keepdims=True)
-                if not diagonal:
-                    old = mrow[kv, 0:1, cols]
-                    top = jnp.maximum(top, old)
-                    factor = jnp.exp2((old - top) * scale)
-                weights = jnp.exp2((scores - top) * scale)
-                total = jnp.sum(weights, axis=0, keepdims=True)
-                update = lax.dot_general(
-                    values, weights.astype(jnp.bfloat16), (((0,), (0,)), ((), ())),
-                    preferred_element_type=jnp.float32,
-                )
-                if not diagonal:
-                    total = total + lrow[kv, 0:1, cols] * factor
-                    update = update + acc[kv, :, cols] * factor
-                mrow[kv, 0:1, cols] = top
-                lrow[kv, 0:1, cols] = total
-                acc[kv, :, cols] = update
+        heads = [(kv, g) for kv in range(kv_local) for g in range(group)]
+        keys_of, values_of = {}, {}
+
+        def scores_of(kv, g):
+            if kv not in keys_of:
+                at = slice(kv * HDIM, (kv + 1) * HDIM)
+                keys_of[kv] = jnp.concatenate([buf[src, 0:rows, at], key_mask], axis=1)
+                values_of[kv] = buf[src, v_at:, at].T
+            scores = jnp.dot(
+                keys_of[kv],
+                qa[kv, :, g * rows : (g + 1) * rows],
+                preferred_element_type=jnp.float32,
+            )
+            if diagonal:
+                key_pos = lax.broadcasted_iota(jnp.int32, scores.shape, 0)
+                query_pos = lax.broadcasted_iota(jnp.int32, scores.shape, 1)
+                scores = jnp.where(key_pos <= query_pos, scores, NEG_MASK)
+            return scores
+
+        ahead = 2
+        ready = [scores_of(*head) for head in heads[:ahead]]
+        for index, (kv, g) in enumerate(heads):
+            cols = slice(g * rows, (g + 1) * rows)
+            scores = ready.pop(0)
+            if index + ahead < len(heads):
+                ready.append(scores_of(*heads[index + ahead]))
+            top = jnp.max(scores, axis=0, keepdims=True)
+            if not diagonal:
+                old = mrow[kv, 0:1, cols]
+                top = jnp.maximum(top, old)
+                factor = jnp.exp2((old - top) * scale)
+            weights = jnp.exp2((scores - top) * scale)
+            total = jnp.sum(weights, axis=0, keepdims=True)
+            update = jnp.dot(
+                values_of[kv], weights.astype(jnp.bfloat16), preferred_element_type=jnp.float32
+            )
+            if not diagonal:
+                total = total + lrow[kv, 0:1, cols] * factor
+                update = update + acc[kv, :, cols] * factor
+            mrow[kv, 0:1, cols] = top
+            lrow[kv, 0:1, cols] = total
+            acc[kv, :, cols] = update
 
     attend(me, True)
 
@@ -264,7 +280,7 @@
 
         @pl.when(held)
         def _():
-            for part in range(2):
+            for part in range(len(parts)):
                 copy(src, part, 0, sibling).wait_recv()
 
                 @pl.when(lax.rem(kind, 2) == 0)
@@ -357,8 +373,8 @@
             pltpu.VMEM((chunks, rows, width), jnp.bfloat16),
             pltpu.VMEM((chunks, rows, width), jnp.float32),
             pltpu.VMEM((chunks, rows, width), jnp.bfloat16),
-            pltpu.SemaphoreType.DMA((3, ctx_size, 2)),
-            pltpu.SemaphoreType.DMA((ctx_size, 2)),
+            pltpu.SemaphoreType.DMA((3, ctx_size, 4)),
+            pltpu.SemaphoreType.DMA((ctx_size, 4)),
             pltpu.SemaphoreType.DMA,
             pltpu.SemaphoreType.DMA((chunks,)),
             pltpu.SemaphoreType.DMA((chunks,)),

time: 110 us -> 89.7 us (0.82)
  Pallas kernels: 103 us -> 82.9 us
    pallas_call x1, Pallas kernels: 103 us -> 82.9 us  [fused_device(): pl.pallas_call(partial(fused_kernel, ctx_size // 4, reach), out_shape=(ja...]
where the time goes in v2:
time: 89.7 us; the launch traced here: 89.4 us
  Pallas kernels  82.9 us (92%)
  local copies, waits for them, and re-layouts  5.26 us (6%)
    pallas_call x1, Pallas kernels, fused_device(): pl.pallas_call(partial(fused_kernel, ctx_size // 4, reach), out_shape=(ja...  82.9 us
    unnamed x6, local copies, waits for them, and re-layouts  5.18 us

profile of v2, /device:TPU:24, one launch (start us, length us, event | category | flops | bytes accessed | tf_op | source)
XLA Modules:
  0.0 89.4 jit_solution(14335024351289541781)
XLA Ops:
  0.6 0.7 convert_element_type.3
  1.3 0.1 scatter.8.doc_ref
  1.4 0.0 copy-start
  1.4 0.9 %copy-done = bf16[256,512]{1,0:T(8,128)(2,1)S(1)} copy-done((bf16[256,512]{1,0:T(8,128)(2,1)S(1)}, bf16[256,512]{1,0:T(8,128)(2,1)}, u32[]{:S(2)}) %copy-start) | copy-done | bytes 262168
  2.3 0.0 copy-start.1
  2.3 0.9 %copy-done.1 = bf16[256,512]{1,0:T(8,128)(2,1)S(1)} copy-done((bf16[256,512]{1,0:T(8,128)(2,1)S(1)}, bf16[256,512]{1,0:T(8,128)(2,1)}, u32[]{:S(2)}) %copy-start.1) | copy-done | bytes 262168
  3.3 82.9 %shard_map.68 = (bf16[256,2048]{1,0:T(8,128)(2,1)S(1)}, bf16[256,2048]{1,0:T(8,128)(2,1)}) custom-call(bf16[256,2048]{1,0:T(8,128)(2,1)} %q_ref.1, bf16[256,512]{1,0:T(8,128)(2,1)S(1)} %copy-done, bf16[256,512]{1,0:T(8,128)(2,1)S(1)} %copy-done.1, bf16[16,512]{1,0:T(8,128)(2,1)S(1)} %scatter.8.doc_ref, bf16[2048,4096]{1,0:T(8,128)(2,1)} %w_ref.1), custom_call_target="tpu_custom_call" | custom-call | tf_op jit(solution)/shard_map/pallas_call | solution.py:358
  86.2 1.0 %copy.9 = bf16[256,2048]{1,0:T(8,128)(2,1)} copy(bf16[256,2048]{1,0:T(8,128)(2,1)S(1)} %get-tuple-element.16) | data formatting | bytes 2097152
  87.1 2.3 %copy.10 = bf16[256,2048]{1,0:T(8,128)(2,1)} copy(bf16[256,2048]{1,0:T(8,128)(2,1)} %get-tuple-element.17) | data formatting | bytes 2097152
  (1 shorter events, 0.0 us)
Async XLA Ops:
  1.4 1.0 %copy-start = (bf16[256,512]{1,0:T(8,128)(2,1)S(1)}, bf16[256,512]{1,0:T(8,128)(2,1)}, u32[]{:S(2)}) copy-start(bf16[256,512]{1,0:T(8,128)(2,1)} %k_ref.1) | copy-start | bytes 786436
  2.3 0.9 %copy-start.1 = (bf16[256,512]{1,0:T(8,128)(2,1)S(1)}, bf16[256,512]{1,0:T(8,128)(2,1)}, u32[]{:S(2)}) copy-start(bf16[256,512]{1,0:T(8,128)(2,1)} %v_ref.1) | copy-start | bytes 786436

commit v3 on v2

--- a/solution.py
+++ b/solution.py
@@ -111,9 +111,9 @@
 
 
 def fused_kernel(
-    levels, reach, q_ref, k_ref, v_ref, doc_ref, w_ref, att_ref, proj_ref,
-    buf, qa, acc, mrow, lrow, wbuf, psend, pown, precv,
-    send_sem, recv_sem, w_sem, ysend_sem, yrecv_sem,
+    levels, reach, q_hbm, k_ref, v_ref, doc_ref, w_ref, att_ref, proj_ref,
+    q_ref, buf, qa, acc, mrow, lrow, wbuf, psend, pown, precv,
+    send_sem, recv_sem, w_sem, in_sem, ysend_sem, yrecv_sem,
 ):
     rows = q_ref.shape[0]
     kv_local = k_ref.shape[1] // HDIM
@@ -126,6 +126,12 @@
     up, across, sibling = me + 4, 4 * z + 2 * (1 - x) + c, 4 * z + 2 * x + (1 - c)
     across_chip = 4 * z + 2 * (1 - x)
 
+    k_copy = pltpu.make_async_copy(k_ref, buf.at[me, pl.ds(0, rows)], in_sem.at[0])
+    v_copy = pltpu.make_async_copy(v_ref, buf.at[me, pl.ds(v_at, rows)], in_sem.at[1])
+    q_copy = pltpu.make_async_copy(q_hbm, q_ref, in_sem.at[2])
+    k_copy.start()
+    v_copy.start()
+    q_copy.start()
     w_copy = pltpu.make_async_copy(w_ref, wbuf, w_sem)
     w_copy.start()
 
@@ -142,9 +148,9 @@
     def _():
         pl.semaphore_signal(barrier, inc=1, device_id={"ctx": me - 4}, device_id_type=MESH)
 
-    buf[me, 0:rows, :] = k_ref[...]
     buf[me, rows:v_at, :] = doc_ref[...]
-    buf[me, v_at:, :] = v_ref[...]
+    k_copy.wait()
+    v_copy.wait()
 
     pl.semaphore_wait(
         barrier, 3 + jnp.where(z + 1 < levels, 1, 0) + jnp.where(z > 0, 1, 0)
@@ -196,6 +202,7 @@
         query_doc = jnp.where(inside, docs[b : b + 1, 0:rows], query_doc)
     ids = lax.broadcasted_iota(jnp.int32, (HDIM, rows), 0).astype(jnp.float32)
     onehot = jnp.where(ids == query_doc, 1.0, 0.0).astype(jnp.bfloat16)
+    q_copy.wait()
     for kv in range(kv_local):
         for g in range(group):
             head = (kv * group + g) * HDIM
@@ -277,15 +284,19 @@
     @pl.loop(0, 4 * (levels + 1))
     def _(step):
         src, kind, held, near = event(step)
-
-        @pl.when(held)
+        next_src, next_kind, next_held, _near = event(step + 1)
+        odd = lax.rem(kind, 2) == 1
+
+        @pl.when(odd & next_held)
+        def _():
+            for part in range(len(parts)):
+                copy(next_src, part, 0, sibling).wait_recv()
+                forward(next_src, next_kind == 0, part)
+
+        @pl.when(odd & held)
         def _():
             for part in range(len(parts)):
                 copy(src, part, 0, sibling).wait_recv()
-
-                @pl.when(lax.rem(kind, 2) == 0)
-                def _():
-                    forward(src, kind == 0, part)
 
         @pl.when(near)
         def _():
@@ -355,15 +366,17 @@
         jnp.broadcast_to(doc_ids.astype(jnp.bfloat16)[:, None], (shard_blocks, kv_cols))
     )
     vmem = pl.BlockSpec(memory_space=pltpu.VMEM)
+    hbm = pl.BlockSpec(memory_space=pltpu.HBM)
     return pl.pallas_call(
         partial(fused_kernel, ctx_size // 4, reach),
         out_shape=(
             jax.ShapeDtypeStruct((rows, q_cols), jnp.bfloat16),
             jax.ShapeDtypeStruct((rows, out_cols), jnp.bfloat16),
         ),
-        in_specs=[vmem] * 4 + [pl.BlockSpec(memory_space=pl.ANY)],
+        in_specs=[hbm, hbm, hbm, vmem, hbm],
         out_specs=(vmem, vmem),
         scratch_shapes=[
+            pltpu.VMEM((rows, q_cols), jnp.bfloat16),
             pltpu.VMEM((ctx_size, 2 * rows + 16, kv_cols), jnp.bfloat16),
             pltpu.VMEM((kv_local, 2 * HDIM, group * rows), jnp.bfloat16),
             pltpu.VMEM((kv_local, HDIM, group * rows), jnp.float32),
@@ -376,11 +389,12 @@
             pltpu.SemaphoreType.DMA((3, ctx_size, 4)),
             pltpu.SemaphoreType.DMA((ctx_size, 4)),
             pltpu.SemaphoreType.DMA,
+            pltpu.SemaphoreType.DMA((3,)),
             pltpu.SemaphoreType.DMA((chunks,)),
             pltpu.SemaphoreType.DMA((chunks,)),
         ],
         compiler_params=pltpu.CompilerParams(
-            collective_id=0, has_side_effects=True, vmem_limit_bytes=52 * 1024 * 1024
+            collective_id=0, has_side_effects=True, vmem_limit_bytes=44 * 1024 * 1024
         ),
     )(query_rows, key_rows, value_rows, doc_tile, out_weight)
 

time: 89.7 us -> 83.9 us (0.935)
  Pallas kernels: 82.9 us -> 77.3 us
    pallas_call x1, Pallas kernels: 82.9 us -> 77.3 us  [fused_device(): pl.pallas_call(partial(fused_kernel, ctx_size // 4, reach), out_shape=(ja...]
    unnamed x6 -> x8, local copies, waits for them, and re-layouts: 5.18 us -> 5.07 us
where the time goes in v3:
time: 83.9 us; the launch traced here: 83.7 us
  Pallas kernels  77.3 us (92%)
  local copies, waits for them, and re-layouts  5.15 us (6%)
    pallas_call x1, Pallas kernels, fused_device(): pl.pallas_call(partial(fused_kernel, ctx_size // 4, reach), out_shape=(ja...  77.3 us
    unnamed x8, local copies, waits for them, and re-layouts  5.07 us

profile of v3, /device:TPU:24, one launch (start us, length us, event | category | flops | bytes accessed | tf_op | source)
XLA Modules:
  0.0 83.7 jit_solution(3735851575164757527)
XLA Ops:
  0.6 0.7 convert_element_type.3
  1.3 0.1 scatter.8.doc_ref
  1.4 0.0 copy-start
  1.4 1.2 %copy-done = bf16[256,2048]{1,0:T(8,128)(2,1)S(1)} copy-done((bf16[256,2048]{1,0:T(8,128)(2,1)S(1)}, bf16[256,2048]{1,0:T(8,128)(2,1)}, u32[]{:S(2)}) %copy-start) | copy-done | bytes 1048600
  2.6 0.0 copy-start.1
  2.6 0.9 %copy-done.1 = bf16[256,512]{1,0:T(8,128)(2,1)S(1)} copy-done((bf16[256,512]{1,0:T(8,128)(2,1)S(1)}, bf16[256,512]{1,0:T(8,128)(2,1)}, u32[]{:S(2)}) %copy-start.1) | copy-done | bytes 262168
  3.5 0.0 copy-start.2
  3.6 0.9 %copy-done.2 = bf16[256,512]{1,0:T(8,128)(2,1)S(1)} copy-done((bf16[256,512]{1,0:T(8,128)(2,1)S(1)}, bf16[256,512]{1,0:T(8,128)(2,1)}, u32[]{:S(2)}) %copy-start.2) | copy-done | bytes 262168
  4.5 77.3 %shard_map.68 = (bf16[256,2048]{1,0:T(8,128)(2,1)S(1)}, bf16[256,2048]{1,0:T(8,128)(2,1)S(1)}) custom-call(bf16[256,2048]{1,0:T(8,128)(2,1)S(1)} %copy-done, bf16[256,512]{1,0:T(8,128)(2,1)S(1)} %copy-done.1, bf16[256,512]{1,0:T(8,128)(2,1)S(1)} %copy-done.2, bf16[16,512]{1,0:T(8,128)(2,1)S(1)} %scatter.8.doc_ref, bf16[2048,4096]{1,0:T(8,128)(2,1)} %w_ref.1), custom_call_target="tpu_custom_call" | custom-call | tf_op jit(solution)/shard_map/pallas_call | solution.py:370
  81.8 1.0 %copy.9 = bf16[256,2048]{1,0:T(8,128)(2,1)} copy(bf16[256,2048]{1,0:T(8,128)(2,1)S(1)} %get-tuple-element.16) | data formatting | bytes 2097152
  82.7 1.0 %copy.10 = bf16[256,2048]{1,0:T(8,128)(2,1)} copy(bf16[256,2048]{1,0:T(8,128)(2,1)S(1)} %get-tuple-element.17) | data formatting | bytes 2097152
  (1 shorter events, 0.0 us)
Async XLA Ops:
  1.4 1.2 %copy-start = (bf16[256,2048]{1,0:T(8,128)(2,1)S(1)}, bf16[256,2048]{1,0:T(8,128)(2,1)}, u32[]{:S(2)}) copy-start(bf16[256,2048]{1,0:T(8,128)(2,1)} %q_hbm.1) | copy-start | bytes 3145732
  2.6 0.9 %copy-start.1 = (bf16[256,512]{1,0:T(8,128)(2,1)S(1)}, bf16[256,512]{1,0:T(8,128)(2,1)}, u32[]{:S(2)}) copy-start(bf16[256,512]{1,0:T(8,128)(2,1)} %k_ref.1) | copy-start | bytes 786436
  3.5 0.9 %copy-start.2 = (bf16[256,512]{1,0:T(8,128)(2,1)S(1)}, bf16[256,512]{1,0:T(8,128)(2,1)}, u32[]{:S(2)}) copy-start(bf16[256,512]{1,0:T(8,128)(2,1)} %v_ref.1) | copy-start | bytes 786436

commit v4 on v3

--- a/solution.py
+++ b/solution.py
@@ -170,24 +170,31 @@
             device_id={"ctx": target}, device_id_type=MESH,
         )
 
-    def sends(src, column):
+    def sends(src, column, part):
+        levels_down = z - lax.div(src, 4)
+        by_column = column & (4 * (z + 1) - src <= reach)
+        crossing = column & (src < across_chip) & (across_chip - src <= reach)
+        if part >= 2:
+            by_other = jnp.logical_not(column) & (levels_down == 2)
+            by_column = (by_column | by_other) & (up - src <= reach)
+            crossing = crossing & (levels_down < 3)
         return (
-            (0, up, column & (z + 1 < levels) & (4 * (z + 1) - src <= reach)),
-            (1, across, column & (src < across_chip) & (across_chip - src <= reach)),
+            (0, up, by_column & (z + 1 < levels)),
+            (1, across, crossing),
             (2, sibling, (sibling > src) & (sibling - src <= reach)),
         )
 
     def forward(src, column, part):
-        for direction, target, needed in sends(src, column):
+        for direction, target, needed in sends(src, column, part):
             @pl.when(needed)
             def _():
                 copy(src, part, direction, target).start()
 
     def drain(src, column):
-        for direction, target, needed in sends(src, column):
-            @pl.when(needed)
-            def _():
-                for part in range(len(parts)):
+        for part in range(len(parts)):
+            for direction, target, needed in sends(src, column, part):
+                @pl.when(needed)
+                def _():
                     copy(src, part, direction, target).wait_send()
 
     always = me >= 0
@@ -284,14 +291,16 @@
     @pl.loop(0, 4 * (levels + 1))
     def _(step):
         src, kind, held, near = event(step)
-        next_src, next_kind, next_held, _near = event(step + 1)
+        next_src, next_kind, next_held, next_near = event(step + 1)
         odd = lax.rem(kind, 2) == 1
 
         @pl.when(odd & next_held)
         def _():
             for part in range(len(parts)):
-                copy(next_src, part, 0, sibling).wait_recv()
-                forward(next_src, next_kind == 0, part)
+                @pl.when(next_near | (part < 2))
+                def _():
+                    copy(next_src, part, 0, sibling).wait_recv()
+                    forward(next_src, next_kind == 0, part)
 
         @pl.when(odd & held)
         def _():

time: 83.9 us -> 78.7 us (0.938)
  Pallas kernels: 77.3 us -> 72.1 us
    pallas_call x1, Pallas kernels: 77.3 us -> 72.1 us  [fused_device(): pl.pallas_call(partial(fused_kernel, ctx_size // 4, reach), out_shape=(ja...]
where the time goes in v4:
time: 78.7 us; the launch traced here: 78.5 us
  Pallas kernels  72.1 us (92%)
  local copies, waits for them, and re-layouts  5.15 us (7%)
    pallas_call x1, Pallas kernels, fused_device(): pl.pallas_call(partial(fused_kernel, ctx_size // 4, reach), out_shape=(ja...  72.1 us
    unnamed x8, local copies, waits for them, and re-layouts  5.07 us

profile of v4, /device:TPU:24, one launch (start us, length us, event | category | flops | bytes accessed | tf_op | source)
XLA Modules:
  0.0 78.5 jit_solution(17243376684583121724)
XLA Ops:
  0.6 0.7 convert_element_type.3
  1.3 0.1 scatter.8.doc_ref
  1.4 0.0 copy-start
  1.4 1.2 %copy-done = bf16[256,2048]{1,0:T(8,128)(2,1)S(1)} copy-done((bf16[256,2048]{1,0:T(8,128)(2,1)S(1)}, bf16[256,2048]{1,0:T(8,128)(2,1)}, u32[]{:S(2)}) %copy-start) | copy-done | bytes 1048600
  2.6 0.0 copy-start.1
  2.6 0.9 %copy-done.1 = bf16[256,512]{1,0:T(8,128)(2,1)S(1)} copy-done((bf16[256,512]{1,0:T(8,128)(2,1)S(1)}, bf16[256,512]{1,0:T(8,128)(2,1)}, u32[]{:S(2)}) %copy-start.1) | copy-done | bytes 262168
  3.5 0.0 copy-start.2
  3.6 0.9 %copy-done.2 = bf16[256,512]{1,0:T(8,128)(2,1)S(1)} copy-done((bf16[256,512]{1,0:T(8,128)(2,1)S(1)}, bf16[256,512]{1,0:T(8,128)(2,1)}, u32[]{:S(2)}) %copy-start.2) | copy-done | bytes 262168
  4.5 72.1 %shard_map.68 = (bf16[256,2048]{1,0:T(8,128)(2,1)S(1)}, bf16[256,2048]{1,0:T(8,128)(2,1)S(1)}) custom-call(bf16[256,2048]{1,0:T(8,128)(2,1)S(1)} %copy-done, bf16[256,512]{1,0:T(8,128)(2,1)S(1)} %copy-done.1, bf16[256,512]{1,0:T(8,128)(2,1)S(1)} %copy-done.2, bf16[16,512]{1,0:T(8,128)(2,1)S(1)} %scatter.8.doc_ref, bf16[2048,4096]{1,0:T(8,128)(2,1)} %w_ref.1), custom_call_target="tpu_custom_call" | custom-call | tf_op jit(solution)/shard_map/pallas_call | solution.py:379
  76.6 1.0 %copy.9 = bf16[256,2048]{1,0:T(8,128)(2,1)} copy(bf16[256,2048]{1,0:T(8,128)(2,1)S(1)} %get-tuple-element.16) | data formatting | bytes 2097152
  77.5 1.0 %copy.10 = bf16[256,2048]{1,0:T(8,128)(2,1)} copy(bf16[256,2048]{1,0:T(8,128)(2,1)S(1)} %get-tuple-element.17) | data formatting | bytes 2097152
  (1 shorter events, 0.0 us)
Async XLA Ops:
  1.4 1.2 %copy-start = (bf16[256,2048]{1,0:T(8,128)(2,1)S(1)}, bf16[256,2048]{1,0:T(8,128)(2,1)}, u32[]{:S(2)}) copy-start(bf16[256,2048]{1,0:T(8,128)(2,1)} %q_hbm.1) | copy-start | bytes 3145732
  2.6 0.9 %copy-start.1 = (bf16[256,512]{1,0:T(8,128)(2,1)S(1)}, bf16[256,512]{1,0:T(8,128)(2,1)}, u32[]{:S(2)}) copy-start(bf16[256,512]{1,0:T(8,128)(2,1)} %k_ref.1) | copy-start | bytes 786436
  3.5 0.9 %copy-start.2 = (bf16[256,512]{1,0:T(8,128)(2,1)S(1)}, bf16[256,512]{1,0:T(8,128)(2,1)}, u32[]{:S(2)}) copy-start(bf16[256,512]{1,0:T(8,128)(2,1)} %v_ref.1) | copy-start | bytes 786436

commit v5 on v4

--- a/solution.py
+++ b/solution.py
@@ -230,12 +230,13 @@
 
         heads = [(kv, g) for kv in range(kv_local) for g in range(group)]
         keys_of, values_of = {}, {}
+        ones = jnp.ones((16, rows), jnp.bfloat16)
 
         def scores_of(kv, g):
             if kv not in keys_of:
                 at = slice(kv * HDIM, (kv + 1) * HDIM)
                 keys_of[kv] = jnp.concatenate([buf[src, 0:rows, at], key_mask], axis=1)
-                values_of[kv] = buf[src, v_at:, at].T
+                values_of[kv] = jnp.concatenate([buf[src, v_at:, at].T, ones], axis=0)
             scores = jnp.dot(
                 keys_of[kv],
                 qa[kv, :, g * rows : (g + 1) * rows],
@@ -260,10 +261,10 @@
                 top = jnp.maximum(top, old)
                 factor = jnp.exp2((old - top) * scale)
             weights = jnp.exp2((scores - top) * scale)
-            total = jnp.sum(weights, axis=0, keepdims=True)
-            update = jnp.dot(
+            summed = jnp.dot(
                 values_of[kv], weights.astype(jnp.bfloat16), preferred_element_type=jnp.float32
             )
+            update, total = summed[0:HDIM], summed[HDIM : HDIM + 1]
             if not diagonal:
                 total = total + lrow[kv, 0:1, cols] * factor
                 update = update + acc[kv, :, cols] * factor
@@ -368,7 +369,7 @@
     group = q_cols // kv_cols
     shard_blocks = rows // BLOCK
     reach = -(-(ctx_size * shard_blocks * 5 // 8 - 1) // shard_blocks)
-    width = 512
+    width = 256
     out_cols = out_weight.shape[1] // 2
     chunks = out_cols // width
     doc_tile = jnp.zeros((16, kv_cols), jnp.bfloat16).at[0:shard_blocks].set(

time: 78.7 us -> 78 us (level)
  Pallas kernels: 72.1 us -> 71.3 us
where the time goes in v5:
time: 78 us; the launch traced here: 77.7 us
  Pallas kernels  71.3 us (91%)
  local copies, waits for them, and re-layouts  5.15 us (7%)
    pallas_call x1, Pallas kernels, fused_device(): pl.pallas_call(partial(fused_kernel, ctx_size // 4, reach), out_shape=(ja...  71.3 us
    unnamed x8, local copies, waits for them, and re-layouts  5.07 us

profile of v5, /device:TPU:24, one launch (start us, length us, event | category | flops | bytes accessed | tf_op | source)
XLA Modules:
  0.0 77.7 jit_solution(13187747233251965145)
XLA Ops:
  0.6 0.7 convert_element_type.3
  1.3 0.1 scatter.8.doc_ref
  1.4 0.0 copy-start
  1.4 1.2 %copy-done = bf16[256,2048]{1,0:T(8,128)(2,1)S(1)} copy-done((bf16[256,2048]{1,0:T(8,128)(2,1)S(1)}, bf16[256,2048]{1,0:T(8,128)(2,1)}, u32[]{:S(2)}) %copy-start) | copy-done | bytes 1048600
  2.6 0.0 copy-start.1
  2.6 0.9 %copy-done.1 = bf16[256,512]{1,0:T(8,128)(2,1)S(1)} copy-done((bf16[256,512]{1,0:T(8,128)(2,1)S(1)}, bf16[256,512]{1,0:T(8,128)(2,1)}, u32[]{:S(2)}) %copy-start.1) | copy-done | bytes 262168
  3.5 0.0 copy-start.2
  3.6 0.9 %copy-done.2 = bf16[256,512]{1,0:T(8,128)(2,1)S(1)} copy-done((bf16[256,512]{1,0:T(8,128)(2,1)S(1)}, bf16[256,512]{1,0:T(8,128)(2,1)}, u32[]{:S(2)}) %copy-start.2) | copy-done | bytes 262168
  4.5 71.3 %shard_map.68 = (bf16[256,2048]{1,0:T(8,128)(2,1)S(1)}, bf16[256,2048]{1,0:T(8,128)(2,1)S(1)}) custom-call(bf16[256,2048]{1,0:T(8,128)(2,1)S(1)} %copy-done, bf16[256,512]{1,0:T(8,128)(2,1)S(1)} %copy-done.1, bf16[256,512]{1,0:T(8,128)(2,1)S(1)} %copy-done.2, bf16[16,512]{1,0:T(8,128)(2,1)S(1)} %scatter.8.doc_ref, bf16[2048,4096]{1,0:T(8,128)(2,1)} %w_ref.1), custom_call_target="tpu_custom_call" | custom-call | tf_op jit(solution)/shard_map/pallas_call | solution.py:380
  75.8 1.0 %copy.9 = bf16[256,2048]{1,0:T(8,128)(2,1)} copy(bf16[256,2048]{1,0:T(8,128)(2,1)S(1)} %get-tuple-element.16) | data formatting | bytes 2097152
  76.8 1.0 %copy.10 = bf16[256,2048]{1,0:T(8,128)(2,1)} copy(bf16[256,2048]{1,0:T(8,128)(2,1)S(1)} %get-tuple-element.17) | data formatting | bytes 2097152
  (1 shorter events, 0.0 us)
Async XLA Ops:
  1.4 1.2 %copy-start = (bf16[256,2048]{1,0:T(8,128)(2,1)S(1)}, bf16[256,2048]{1,0:T(8,128)(2,1)}, u32[]{:S(2)}) copy-start(bf16[256,2048]{1,0:T(8,128)(2,1)} %q_hbm.1) | copy-start | bytes 3145732
  2.6 0.9 %copy-start.1 = (bf16[256,512]{1,0:T(8,128)(2,1)S(1)}, bf16[256,512]{1,0:T(8,128)(2,1)}, u32[]{:S(2)}) copy-start(bf16[256,512]{1,0:T(8,128)(2,1)} %k_ref.1) | copy-start | bytes 786436
  3.5 0.9 %copy-start.2 = (bf16[256,512]{1,0:T(8,128)(2,1)S(1)}, bf16[256,512]{1,0:T(8,128)(2,1)}, u32[]{:S(2)}) copy-start(bf16[256,512]{1,0:T(8,128)(2,1)} %v_ref.1) | copy-start | bytes 786436

commit v6 on v5

--- a/solution.py
+++ b/solution.py
@@ -312,13 +312,12 @@
         def _():
             attend(src, False)
 
-    @pl.loop(0, kv_local)
-    def _(kv):
+    for kv in range(kv_local):
         for g in range(group):
             cols = slice(g * rows, (g + 1) * rows)
-            head = acc[kv, :, cols] / lrow[kv, 0:1, cols]
-            at = pl.ds(pl.multiple_of((kv * group + g) * HDIM, HDIM), HDIM)
-            att_ref[:, at] = head.T.astype(jnp.bfloat16)
+            head = acc[kv, :, cols] * (1.0 / lrow[kv, 0:1, cols])
+            at = (kv * group + g) * HDIM
+            att_ref[:, at : at + HDIM] = head.T.astype(jnp.bfloat16)
 
     w_copy.wait()
     chunks, _, width = psend.shape

time: 78 us -> 77.6 us (level)
  no operation moved by 1% of the time
where the time goes in v6:
time: 77.6 us; the launch traced here: 77.4 us
  Pallas kernels  71 us (91%)
  local copies, waits for them, and re-layouts  5.15 us (7%)
    pallas_call x1, Pallas kernels, fused_device(): pl.pallas_call(partial(fused_kernel, ctx_size // 4, reach), out_shape=(ja...  71 us
    unnamed x8, local copies, waits for them, and re-layouts  5.07 us

profile of v6, /device:TPU:24, one launch (start us, length us, event | category | flops | bytes accessed | tf_op | source)
XLA Modules:
  0.0 77.4 jit_solution(10233737928469169678)
XLA Ops:
  0.6 0.7 convert_element_type.3
  1.3 0.1 scatter.8.doc_ref
  1.4 0.0 copy-start
  1.4 1.2 %copy-done = bf16[256,2048]{1,0:T(8,128)(2,1)S(1)} copy-done((bf16[256,2048]{1,0:T(8,128)(2,1)S(1)}, bf16[256,2048]{1,0:T(8,128)(2,1)}, u32[]{:S(2)}) %copy-start) | copy-done | bytes 1048600
  2.6 0.0 copy-start.1
  2.6 0.9 %copy-done.1 = bf16[256,512]{1,0:T(8,128)(2,1)S(1)} copy-done((bf16[256,512]{1,0:T(8,128)(2,1)S(1)}, bf16[256,512]{1,0:T(8,128)(2,1)}, u32[]{:S(2)}) %copy-start.1) | copy-done | bytes 262168
  3.5 0.0 copy-start.2
  3.6 0.9 %copy-done.2 = bf16[256,512]{1,0:T(8,128)(2,1)S(1)} copy-done((bf16[256,512]{1,0:T(8,128)(2,1)S(1)}, bf16[256,512]{1,0:T(8,128)(2,1)}, u32[]{:S(2)}) %copy-start.2) | copy-done | bytes 262168
  4.5 71.0 %shard_map.68 = (bf16[256,2048]{1,0:T(8,128)(2,1)S(1)}, bf16[256,2048]{1,0:T(8,128)(2,1)S(1)}) custom-call(bf16[256,2048]{1,0:T(8,128)(2,1)S(1)} %copy-done, bf16[256,512]{1,0:T(8,128)(2,1)S(1)} %copy-done.1, bf16[256,512]{1,0:T(8,128)(2,1)S(1)} %copy-done.2, bf16[16,512]{1,0:T(8,128)(2,1)S(1)} %scatter.8.doc_ref, bf16[2048,4096]{1,0:T(8,128)(2,1)} %w_ref.1), custom_call_target="tpu_custom_call" | custom-call | tf_op jit(solution)/shard_map/pallas_call | solution.py:379
  75.5 1.0 %copy.9 = bf16[256,2048]{1,0:T(8,128)(2,1)} copy(bf16[256,2048]{1,0:T(8,128)(2,1)S(1)} %get-tuple-element.16) | data formatting | bytes 2097152
  76.4 1.0 %copy.10 = bf16[256,2048]{1,0:T(8,128)(2,1)} copy(bf16[256,2048]{1,0:T(8,128)(2,1)S(1)} %get-tuple-element.17) | data formatting | bytes 2097152
  (1 shorter events, 0.0 us)
Async XLA Ops:
  1.4 1.2 %copy-start = (bf16[256,2048]{1,0:T(8,128)(2,1)S(1)}, bf16[256,2048]{1,0:T(8,128)(2,1)}, u32[]{:S(2)}) copy-start(bf16[256,2048]{1,0:T(8,128)(2,1)} %q_hbm.1) | copy-start | bytes 3145732
  2.6 0.9 %copy-start.1 = (bf16[256,512]{1,0:T(8,128)(2,1)S(1)}, bf16[256,512]{1,0:T(8,128)(2,1)}, u32[]{:S(2)}) copy-start(bf16[256,512]{1,0:T(8,128)(2,1)} %k_ref.1) | copy-start | bytes 786436
  3.5 0.9 %copy-start.2 = (bf16[256,512]{1,0:T(8,128)(2,1)S(1)}, bf16[256,512]{1,0:T(8,128)(2,1)}, u32[]{:S(2)}) copy-start(bf16[256,512]{1,0:T(8,128)(2,1)} %v_ref.1) | copy-start | bytes 786436
